TPU v7x, 256 devices: a whole 4x4x8 slice. The times are simulated.
256 devices in a mesh: eig: 16 (over x, z_hi, core), store: 16 (over z_lo, y).
Axes of the slice: x: 4, y: 4, z: 8 (z_hi: 2, z_lo: 4; z = z_hi * 4 + z_lo), core: 2. Of those that a mesh axis runs over, the one named last changes fastest.
Arguments:
- acts: bfloat16 [2048, 8192], P('store'), may hold values from -6 to 6
- basis: bfloat16 [8192, 8192], P('store', 'eig'), may hold values from -0.0625 to 0.0625
- eigvals: float32 [64, 8192], P(None, 'eig'), may hold values from 0.5 to 8
- projection: bfloat16 [8192, 64], P('eig'), may hold values from -0.0625 to 0.0625
- out_factor: float32 [2048, 64], P('store', 'eig'), may hold values from -6 to 6
- store: bfloat16 [32768, 4096], P('store', 'eig'), may hold values from -0.09375 to 0.09375
Outputs:
- scores: float32 [2048, 32768], P(None, ('store', 'eig'))
All inputs are finite; a program needn't handle non-finite values.
Results may differ from a plain program's by a relative error of at most 0.0041.
Values may be sent and summed in bfloat16 or wider, within the bound.
A program may use at most 64 MiB of HBM per device.

v0:
```python
import jax
import jax.numpy as jnp
from jax import lax
from jax.sharding import PartitionSpec as P

K_OUT = 64
K_IN = 64
damping = 0.1


def joined_along(blocks, dim):
    blocks = jnp.moveaxis(blocks, 0, dim)
    shape = blocks.shape
    return blocks.reshape(*shape[:dim], shape[dim] * shape[dim + 1], *shape[dim + 2 :])


def from_everyone(shard, axis):
    copies = jnp.broadcast_to(shard, (lax.axis_size(axis), *shard.shape))
    return lax.all_to_all(copies, axis, split_axis=0, concat_axis=0, tiled=True)


def gathered_copies(shard, axis, dim):
    return joined_along(from_everyone(shard, axis), dim)


def body(acts, basis, eigvals, projection, out_factor, store):
    queries = acts.shape[0]
    columns = basis.shape[1]
    rotated = jnp.dot(
        acts, lax.all_gather(basis, "store", axis=0, tiled=True), preferred_element_type=jnp.float32
    )
    inverse = 1.0 / (eigvals + damping)
    scaled = (rotated[:, None, :] * inverse[None, :, :]).astype(jnp.bfloat16)
    partial_value = jnp.dot(
        scaled.reshape(queries * K_OUT, columns), projection, preferred_element_type=jnp.float32
    )
    partial_value = partial_value.reshape(queries, K_OUT * K_IN)
    summed = lax.psum_scatter(partial_value, "eig", scatter_dimension=1, tiled=True)
    kept = out_factor.shape[1]
    features = (summed.reshape(queries, kept, K_IN) * out_factor[:, :, None]).reshape(
        queries, kept * K_IN
    )
    features = features.astype(jnp.bfloat16)
    partial_scores = jnp.einsum(
        "qf,rf->qr",
        gathered_copies(features, "store", 0),
        store,
        preferred_element_type=jnp.float32,
    )
    return lax.psum_scatter(partial_scores, "eig", scatter_dimension=1, tiled=True)


def solution(mesh):
    placed = (
        P("store", None),
        P("store", "eig"),
        P(None, "eig"),
        P("eig", None),
        P("store", "eig"),
        P("store", "eig"),
    )
    return jax.shard_map(
        body, mesh=mesh, in_specs=placed, out_specs=P(None, ("store", "eig")), check_vma=False
    )
```

profile of v0, /device:TPU:1, one launch (start us, length us, event | category | flops | bytes accessed | tf_op | source)
XLA Modules:
  0.0 479.9 jit_solution(4561740160038415110)
XLA Ops:
  6.5 0.0 copy-start
  6.5 0.0 all-gather.2.cloned.1.call-start
  6.5 0.7 all-gather.2.cloned.1.call-update
  7.3 0.0 reduce-scatter.3.cloned.1.call-start
  7.3 0.9 add_divide_fusion
  8.2 107.2 %all-gather.2.cloned.1.call-done = bf16[8192,512]{1,0:T(8,128)(2,1)} async-done(((bf16[512,512]{1,0:T(8,128)(2,1)}), bf16[8192,512]{1,0:T(8,128)(2,1)}) %all-gather.2.cloned.1.call-update) | async-done | bytes 8388624 | tf_op jit(solution)/shard_map/all_gather | solution.py:30
  115.5 0.0 copy-done
  115.5 4.6 fusion
  120.1 0.0 copy-start.2
  120.1 3.4 multiply_convert_fusion
  123.5 0.0 copy-done.2
  123.5 4.3 fusion.1
  127.8 0.0 copy-start.3
  127.8 0.0 copy-start.1
  127.8 4.8 %reshape.17 = f32[128,4096]{1,0:T(8,128)} reshape(f32[8192,64]{1,0:T(8,128)} %fusion.1) | data formatting | bytes 4194304 | tf_op jit(solution)/shard_map/reshape | solution.py:37
  132.6 0.0 reduce-scatter.3.cloned.1.call-update
  132.6 0.0 reduce-scatter.5.cloned.1.call-start
  132.7 0.0 copy-done.3
  132.7 0.1 copy.9
  132.8 82.8 %reduce-scatter.3.cloned.1.call-done = f32[128,256]{1,0:T(8,128)} async-done(((f32[128,4096]{1,0:T(8,128)}), f32[128,256]{1,0:T(8,128)}) %reduce-scatter.3.cloned.1.call-update) | async-done | bytes 131088 | tf_op jit(solution)/shard_map/reduce_scatter | solution.py:38
  215.6 0.9 multiply_convert_fusion.1
  216.5 0.1 broadcast_in_dim.2
  216.6 28.1 %all_to_all.5 = bf16[16,128,256]{2,1,0:T(8,128)(2,1)S(1)} all-to-all(bf16[16,128,256]{2,1,0:T(8,128)(2,1)S(1)} %broadcast_in_dim.2), channel_id=1, replica_groups=mesh['eig'=16,'store'=16] {'store'}, dimensions={0} | all-to-all | bytes 2097152 | tf_op jit(solution)/shard_map/all_to_all | solution.py:19
  244.7 0.0 copy-done.1
  244.7 8.1 %fusion.2 = f32[2048,2048]{1,0:T(8,128)} fusion(bf16[2048,256]{1,0:T(8,128)(2,1)S(1)} %bitcast.10, bf16[2048,256]{1,0:T(8,128)(2,1)S(1)} %copy-done.1), kind=kOutput, calls=%fused_computation.5 | convolution fusion | flops 2147483648 | bytes 18874368 | tf_op jit(solution)/shard_map/qf,rf->qr/dot_general | solution.py:44
  252.8 0.0 reduce-scatter.5.cloned.1.call-update
  252.8 220.6 %reduce-scatter.5.cloned.1.call-done = f32[2048,128]{1,0:T(8,128)} async-done(((f32[2048,2048]{1,0:T(8,128)}), f32[2048,128]{1,0:T(8,128)}) %reduce-scatter.5.cloned.1.call-update) | async-done | bytes 1048592 | tf_op jit(solution)/shard_map/reduce_scatter | solution.py:50
  (1 shorter events, 0.0 us)
Async XLA Ops:
  6.5 108.9 %copy-start = (bf16[128,8192]{1,0:T(8,128)(2,1)S(1)}, bf16[128,8192]{1,0:T(8,128)(2,1)}, u32[]{:S(2)}) copy-start(bf16[128,8192]{1,0:T(8,128)(2,1)} %param.6) | copy-start | bytes 6291460
  6.5 108.9 %all-gather.2.cloned.1.call-start = ((), (), s32[]{:S(2)}) async-start(), calls=%async_computation.3 | async-start | bytes 8912896 | tf_op jit(solution)/shard_map/all_gather | solution.py:30
  7.3 208.3 %reduce-scatter.3.cloned.1.call-start = ((), (), s32[]{:S(2)}) async-start(), calls=%async_computation.4 | async-start | bytes 2228224 | tf_op jit(solution)/shard_map/reduce_scatter | solution.py:38
  120.1 3.4 copy-start.2
  127.8 4.9 %copy-start.3 = (f32[128,4]{0,1:T(4,128)S(1)}, f32[128,4]{0,1:T(4,128)}, u32[]{:S(2)}) copy-start(f32[128,4]{0,1:T(4,128)} %param.10) | copy-start | bytes 6148
  127.8 116.9 %copy-start.1 = (bf16[2048,256]{1,0:T(8,128)(2,1)S(1)}, bf16[2048,256]{1,0:T(8,128)(2,1)}, u32[]{:S(2)}) copy-start(bf16[2048,256]{1,0:T(8,128)(2,1)} %param.11) | copy-start | bytes 3145732
  132.6 340.8 %reduce-scatter.5.cloned.1.call-start = ((), (), s32[]{:S(2)}) async-start(), calls=%async_computation.5 | async-start | bytes 17825792 | tf_op jit(solution)/shard_map/reduce_scatter | solution.py:50
Sparse Core Ops, SparseCore 0:
  9.1 106.2 all-gather.1
  132.8 82.7 reduce-scatter.2
  252.9 220.4 reduce-scatter.4
where the time goes:
time: 480 us
  waiting for transfers between devices  411 us (86%)
  blocking collectives  28.1 us (6%)
  matrix products  17 us (4%)
  between operations  13.2 us (3%)
  other arithmetic  5.2 us (1%)
  local copies, waits for them, and re-layouts  5.06 us (1%)
    reduce_scatter x1, waiting for transfers between devices, body(): lax.psum_scatter(partial_scores, 'eig', scatter_dimension=1, tiled=True)  221 us
    all_gather x1, waiting for transfers between devices, body(): lax.all_gather(basis, 'store', axis=0, tiled=True)  107 us
    reduce_scatter x1, waiting for transfers between devices, body(): lax.psum_scatter(partial_value, 'eig', scatter_dimension=1, tiled=True)  82.8 us
    all_to_all x1, blocking collectives, from_everyone(): return lax.all_to_all(copies, axis, split_axis=0, concat_axis=0, tiled=True)  28.1 us
  transfers between devices with their start and end apart: 3, of which 3 were waited for; matrix products, arithmetic and copies ran while one was open for 0% of the time, Pallas kernels for 0%

commit v1 on v0

--- a/solution.py
+++ b/solution.py
@@ -6,6 +6,15 @@
 K_OUT = 64
 K_IN = 64
 damping = 0.1
+
+
+def read_inputs_now(content, link_axis):
+    return jnp.concatenate(
+        lax.all_to_all(
+            jnp.stack([content for _ in range(lax.axis_size(link_axis))]), link_axis, 0, 0
+        ),
+        0,
+    )
 
 
 def joined_along(blocks, dim):
@@ -26,9 +35,7 @@
 def body(acts, basis, eigvals, projection, out_factor, store):
     queries = acts.shape[0]
     columns = basis.shape[1]
-    rotated = jnp.dot(
-        acts, lax.all_gather(basis, "store", axis=0, tiled=True), preferred_element_type=jnp.float32
-    )
+    rotated = jnp.dot(acts, read_inputs_now(basis, "store"), preferred_element_type=jnp.float32)
     inverse = 1.0 / (eigvals + damping)
     scaled = (rotated[:, None, :] * inverse[None, :, :]).astype(jnp.bfloat16)
     partial_value = jnp.dot(

time: 480 us -> 573 us (1.19)
  waiting for transfers between devices: 411 us -> 490 us
  starting transfers between devices: 0.08 us -> 9.45 us
    all_to_all x0 -> x1, waiting for transfers between devices: none -> 151 us  [read_inputs_now(): lax.all_to_all(jnp.stack([content for _ in range(lax.axis_size(link_axis)...]
    all_gather x1 -> x0, waiting for transfers between devices: 107 us -> none  [body(): lax.all_gather(basis, 'store', axis=0, tiled=True)]
    reduce_scatter x1, waiting for transfers between devices: 82.8 us -> 118 us  [body(): lax.psum_scatter(partial_value, 'eig', scatter_dimension=1, tiled=True)]
    all_to_all x0 -> x1, starting transfers between devices: none -> 9.37 us  [read_inputs_now(): lax.all_to_all(jnp.stack([content for _ in range(lax.axis_size(link_axis)...]
where the time goes in v1:
time: 573 us; the launch traced here: 572 us
  waiting for transfers between devices  490 us (86%)
  blocking collectives  28.1 us (5%)
  matrix products  17 us (3%)
  between operations  13.5 us (2%)
  local copies, waits for them, and re-layouts  10.3 us (2%)
  starting transfers between devices  9.45 us (2%)
    reduce_scatter x1, waiting for transfers between devices, body(): lax.psum_scatter(partial_scores, 'eig', scatter_dimension=1, tiled=True)  220 us
    all_to_all x1, waiting for transfers between devices, read_inputs_now(): lax.all_to_all(jnp.stack([content for _ in range(lax.axis_size(link_axis)...  151 us
    reduce_scatter x1, waiting for transfers between devices, body(): lax.psum_scatter(partial_value, 'eig', scatter_dimension=1, tiled=True)  118 us
    all_to_all x1, blocking collectives, from_everyone(): return lax.all_to_all(copies, axis, split_axis=0, concat_axis=0, tiled=True)  28.1 us
  transfers between devices with their start and end apart: 3, of which 3 were waited for; matrix products, arithmetic and copies ran while one was open for 0% of the time, Pallas kernels for 0%

profile of v1, /device:TPU:1, one launch (start us, length us, event | category | flops | bytes accessed | tf_op | source)
XLA Modules:
  0.0 572.4 jit_solution(16063353743082047149)
XLA Ops:
  6.5 0.0 copy-start
  6.5 5.2 stack.2
  11.8 0.0 copy-start.2
  11.8 9.4 %all-to-all-start = ((bf16[16,512,512]{2,1,0:T(8,128)(2,1)}), bf16[16,512,512]{2,1,0:T(8,128)(2,1)}, u32[]{:S(2)}, u32[]{:S(2)}) async-start(bf16[16,512,512]{2,1,0:T(8,128)(2,1)} %stack.2), calls=%async_computation | async-start | bytes 16777216 | tf_op jit(solution)/shard_map/all_to_all | solution.py:13
  21.1 0.0 reduce-scatter.3.cloned.1.call-start
  21.2 0.0 copy-done.2
  21.2 151.2 %all-to-all-done = bf16[16,512,512]{2,1,0:T(8,128)(2,1)} async-done(((bf16[16,512,512]{2,1,0:T(8,128)(2,1)}), bf16[16,512,512]{2,1,0:T(8,128)(2,1)}, u32[]{:S(2)}, u32[]{:S(2)}) %all-to-all-start) | async-done | bytes 8388640 | tf_op jit(solution)/shard_map/all_to_all | solution.py:13
  172.4 0.0 copy-done
  172.4 4.6 fusion
  177.0 0.0 copy-start.3
  177.0 3.4 multiply_convert_fusion
  180.4 0.0 copy-done.3
  180.4 4.3 fusion.1
  184.7 0.0 copy-start.4
  184.7 0.0 copy-start.1
  184.7 4.8 reshape.23
  189.5 0.0 reduce-scatter.3.cloned.1.call-update
  189.6 0.0 reduce-scatter.5.cloned.1.call-start
  189.6 0.0 copy-done.4
  189.6 0.1 copy.9
  189.7 118.1 %reduce-scatter.3.cloned.1.call-done = f32[128,256]{1,0:T(8,128)} async-done(((f32[128,4096]{1,0:T(8,128)}), f32[128,256]{1,0:T(8,128)}) %reduce-scatter.3.cloned.1.call-update) | async-done | bytes 131088 | tf_op jit(solution)/shard_map/reduce_scatter | solution.py:45
  307.9 0.9 multiply_convert_fusion.1
  308.8 0.1 broadcast_in_dim.2
  308.9 28.1 %all_to_all.10 = bf16[16,128,256]{2,1,0:T(8,128)(2,1)S(1)} all-to-all(bf16[16,128,256]{2,1,0:T(8,128)(2,1)S(1)} %broadcast_in_dim.2), channel_id=1, replica_groups=mesh['eig'=16,'store'=16] {'store'}, dimensions={0} | all-to-all | bytes 2097152 | tf_op jit(solution)/shard_map/all_to_all | solution.py:28
  337.0 0.0 copy-done.1
  337.0 8.1 %fusion.2 = f32[2048,2048]{1,0:T(8,128)} fusion(bf16[2048,256]{1,0:T(8,128)(2,1)S(1)} %bitcast.11, bf16[2048,256]{1,0:T(8,128)(2,1)S(1)} %copy-done.1), kind=kOutput, calls=%fused_computation.5 | convolution fusion | flops 2147483648 | bytes 18874368 | tf_op jit(solution)/shard_map/qf,rf->qr/dot_general | solution.py:51
  345.1 0.0 reduce-scatter.5.cloned.1.call-update
  345.1 220.5 %reduce-scatter.5.cloned.1.call-done = f32[2048,128]{1,0:T(8,128)} async-done(((f32[2048,2048]{1,0:T(8,128)}), f32[2048,128]{1,0:T(8,128)}) %reduce-scatter.5.cloned.1.call-update) | async-done | bytes 1048592 | tf_op jit(solution)/shard_map/reduce_scatter | solution.py:57
  (2 shorter events, 0.0 us)
Async XLA Ops:
  6.5 165.9 %copy-start = (bf16[128,8192]{1,0:T(8,128)(2,1)S(1)}, bf16[128,8192]{1,0:T(8,128)(2,1)}, u32[]{:S(2)}) copy-start(bf16[128,8192]{1,0:T(8,128)(2,1)} %param.6) | copy-start | bytes 6291460
  11.8 9.4 %copy-start.2 = (f32[64,512]{1,0:T(8,128)S(1)}, f32[64,512]{1,0:T(8,128)}, u32[]{:S(2)}) copy-start(f32[64,512]{1,0:T(8,128)} %param.8) | copy-start | bytes 393220
  11.8 160.6 %all-to-all-start = ((bf16[16,512,512]{2,1,0:T(8,128)(2,1)}), bf16[16,512,512]{2,1,0:T(8,128)(2,1)}, u32[]{:S(2)}, u32[]{:S(2)}) async-start(bf16[16,512,512]{2,1,0:T(8,128)(2,1)} %stack.2), calls=%async_computation | async-start | bytes 16777216 | tf_op jit(solution)/shard_map/all_to_all | solution.py:13
  21.1 286.7 %reduce-scatter.3.cloned.1.call-start = ((), (), s32[]{:S(2)}) async-start(), calls=%async_computation.4 | async-start | bytes 2228224 | tf_op jit(solution)/shard_map/reduce_scatter | solution.py:45
  177.0 3.4 copy-start.3
  184.7 4.9 copy-start.4
  184.7 152.3 %copy-start.1 = (bf16[2048,256]{1,0:T(8,128)(2,1)S(1)}, bf16[2048,256]{1,0:T(8,128)(2,1)}, u32[]{:S(2)}) copy-start(bf16[2048,256]{1,0:T(8,128)(2,1)} %param.11) | copy-start | bytes 3145732
  189.6 376.0 %reduce-scatter.5.cloned.1.call-start = ((), (), s32[]{:S(2)}) async-start(), calls=%async_computation.5 | async-start | bytes 17825792 | tf_op jit(solution)/shard_map/reduce_scatter | solution.py:57
Sparse Core Ops, SparseCore 0:
  189.7 118.1 reduce-scatter.2
  345.2 220.3 reduce-scatter.4
